TPU v7x, 512 devices: a whole 4x4x16 slice. The times are simulated.
512 devices in a mesh: row: 32 (over z_lo, y), col: 16 (over z_hi, x, core).
Axes of the slice: x: 4, y: 4, z: 16 (z_hi: 2, z_lo: 8; z = z_hi * 8 + z_lo), core: 2. Of those that a mesh axis runs over, the one named last changes fastest.
Arguments:
- entries: int32 [128, 64, 128, 128], P('row', 'col'), may hold values from -2 to 2
- tile_cols: int32 [128, 64], P('row', 'col'), may hold values from 0 to 31
- block_now: int32 [32, 65536], P(None, ('col', 'row')), may hold values from 0 to 65520
- block_prev: int32 [32, 65536], P(None, ('col', 'row')), may hold values from 0 to 65520
- block_prev2: int32 [32, 65536], P(None, ('col', 'row')), may hold values from 0 to 65520
- gram_prev: int32 [32, 32], replicated, may hold values from 0 to 65520
- square_prev: int32 [32, 32], replicated, may hold values from 0 to 65520
- inverse_prev: int32 [32, 32], replicated, may hold values from 0 to 65520
- inverse_prev2: int32 [32, 32], replicated, may hold values from 0 to 65520
Outputs:
- next_block: float32 [32, 65536], P(None, ('col', 'row'))
- later_block: float32 [32, 65536], P(None, ('col', 'row'))
Inputs may be any that keep to these rules, and one draw needn't show every extreme that they name: `tile_cols`: stored tiles that name the same tile column in one tile row add. `block_prev`: residues. `block_prev2`: residues. `gram_prev`: residues. `square_prev`: residues. `inverse_prev`: residues. `inverse_prev2`: residues.
All inputs are finite; a program needn't handle non-finite values.
Results may differ from a plain program's by a relative error of at most 0.0003.
Values sent between devices are 32-bit elements; how exact they have to be, the bound alone decides.
No kernel may reach another device: no remote copies, remote signals or barrier semaphores. Data moves between devices by JAX's collectives and lax.ppermute only.
A program may use at most 64 MiB of HBM per device.

v0:
```python
import jax
import jax.numpy as jnp
from jax import lax
from jax.sharding import PartitionSpec as P

modulus = 65521.0


def residue(values):
    return jnp.mod(values, modulus)


def split_digits(values):
    top_part = jnp.floor(values / 256.0)
    return (top_part, values - top_part * 256.0)


def fold_digits(top_sum, low_sum):
    return residue(residue(residue(top_sum) * 256.0) + residue(low_sum))


def fold_three(upper_part, middle, lower_part):
    return residue(
        residue(residue(upper_part) * 15.0) + residue(residue(middle) * 256.0) + residue(lower_part)
    )


def mulmod(left_side, right_side):
    top_part, low_part = split_digits(right_side)
    return fold_digits(left_side * top_part, left_side * low_part)


def exact_dot(left_side, right_side):
    return jnp.dot(
        left_side, right_side, precision=lax.Precision.HIGHEST, preferred_element_type=jnp.float32
    )


def small_product(left_side, right_side):
    left_top, left_low = split_digits(left_side)
    right_top, right_low = split_digits(right_side)
    return fold_three(
        exact_dot(left_top, right_top),
        exact_dot(left_top, right_low) + exact_dot(left_low, right_top),
        exact_dot(left_low, right_low),
    )


def inverse_scalar(number):
    result = jnp.ones_like(number)
    square = number
    exponent = 65519
    for position in range(16):
        if exponent >> position & 1:
            result = mulmod(result, square)
        square = mulmod(square, square)
    return result


def inverse_matrix(matrix):
    matrix_order = matrix.shape[0]
    augmented = jnp.concatenate([matrix, jnp.eye(matrix_order, dtype=matrix.dtype)], axis=1)
    row_numbers = jnp.arange(matrix_order, dtype=jnp.int32)

    def eliminate(column, augmented):
        column = jnp.asarray(column).astype(jnp.int32)
        pivot_column = augmented[:, column]
        usable = (pivot_column != 0.0) & (row_numbers >= column)
        pivot_row_id = jnp.where(jnp.any(usable), jnp.argmax(usable), column)
        pivot_row = augmented[pivot_row_id]
        current_row = augmented[column]
        swapped = jnp.where(
            (row_numbers == column)[:, None],
            pivot_row[None, :],
            jnp.where((row_numbers == pivot_row_id)[:, None], current_row[None, :], augmented),
        )
        scaled = mulmod(pivot_row, inverse_scalar(pivot_row[column]))
        factors = jnp.where(row_numbers == column, 0.0, swapped[:, column])
        reduced = residue(swapped - mulmod(factors[:, None], scaled[None, :]) + modulus)
        return jnp.where((row_numbers == column)[:, None], scaled[None, :], reduced)

    augmented = lax.fori_loop(0, matrix_order, eliminate, augmented)
    return augmented[:, matrix_order:]


def coefficients(
    gram_now, square_now, inverse_now, inverse_prev, inverse_prev2, gram_old, square_old
):
    identity = jnp.eye(gram_now.shape[0], dtype=gram_now.dtype)
    first = residue(identity - small_product(residue(square_now + gram_now), inverse_now) + modulus)
    second = residue(modulus - small_product(gram_now, inverse_prev))
    middle = residue(identity - small_product(inverse_prev, gram_old) + modulus)
    third = residue(
        modulus
        - small_product(small_product(residue(square_old + gram_old), middle), inverse_prev2)
    )
    return jnp.concatenate([first, second, third], axis=1)


def digit_stack(values):
    top_part, low_part = split_digits(values)
    return jnp.stack([top_part, low_part]).astype(jnp.bfloat16)


def combine_blocks(coeffs, stacked):
    products = jnp.einsum(
        "dab,ebn->dean",
        digit_stack(coeffs),
        digit_stack(stacked),
        preferred_element_type=jnp.float32,
    )
    return fold_three(products[0, 0], products[0, 1] + products[1, 0], products[1, 1])


def gram_local(first, second):
    column_count = first.shape[1]
    group_width = min(column_count, 128)
    groups = column_count // group_width
    first_digits = digit_stack(first).reshape(2, first.shape[0], groups, group_width)
    second_digits = digit_stack(second).reshape(2, second.shape[0], groups, group_width)
    products = jnp.einsum(
        "dagw,ecgw->gdeac", first_digits, second_digits, preferred_element_type=jnp.float32
    )
    per_group = fold_three(
        products[:, 0, 0], products[:, 0, 1] + products[:, 1, 0], products[:, 1, 1]
    )
    return residue(jnp.sum(per_group, axis=0))


def digit_pair(values):
    top_part, low_part = split_digits(values)
    return jnp.stack([top_part, low_part])


def forward_partial(block_full, tile_values, tile_cols):
    tile_rows, slot_count, tile_size = (
        tile_values.shape[0],
        tile_values.shape[1],
        tile_values.shape[2],
    )
    block_rows = block_full.shape[0]
    top_part, low_part = split_digits(block_full)
    digits = jnp.concatenate([top_part, low_part], axis=0).astype(jnp.bfloat16)
    digits = digits.reshape(2 * block_rows, -1, tile_size)
    picked = jnp.take(digits, tile_cols.reshape(-1), axis=1).reshape(
        2 * block_rows, tile_rows, slot_count, tile_size
    )
    raw_sums = jnp.einsum("brsk,rsjk->brj", picked, tile_values, preferred_element_type=jnp.float32)
    return fold_digits(raw_sums[:block_rows], raw_sums[block_rows:]).reshape(
        block_rows, tile_rows * tile_size
    )


def backward_partial(projected, tile_values, onehot):
    tile_rows, tile_size = (tile_values.shape[0], tile_values.shape[2])
    block_rows = projected.shape[0]
    top_part, low_part = split_digits(projected)
    digits = (
        jnp.concatenate([top_part, low_part], axis=0)
        .astype(jnp.bfloat16)
        .reshape(2 * block_rows, tile_rows, tile_size)
    )
    spread = jnp.einsum("brj,rsjk->brsk", digits, tile_values, preferred_element_type=jnp.float32)
    raw_sums = jnp.einsum(
        "brsk,rsc->bck",
        spread,
        onehot,
        precision=lax.Precision.HIGHEST,
        preferred_element_type=jnp.float32,
    )
    return fold_digits(raw_sums[:block_rows], raw_sums[block_rows:]).reshape(block_rows, -1)


def body(
    entries,
    tile_cols,
    block_now,
    block_prev,
    block_prev2,
    gram_prev,
    square_prev,
    inverse_prev,
    inverse_prev2,
):
    tile_values = entries.astype(jnp.bfloat16)
    tile_size = tile_values.shape[2]
    share_width = block_now.shape[1]
    col_tiles = share_width * lax.axis_size("row") // tile_size
    onehot = (
        tile_cols[:, :, None] == jnp.arange(col_tiles, dtype=jnp.int32)[None, None, :]
    ).astype(jnp.float32)
    current = block_now.astype(jnp.float32)
    earlier = block_prev.astype(jnp.float32)
    earliest = block_prev2.astype(jnp.float32)
    gram_old = gram_prev.astype(jnp.float32)
    square_old = square_prev.astype(jnp.float32)
    inverse_old = inverse_prev.astype(jnp.float32)
    inverse_older = inverse_prev2.astype(jnp.float32)
    results = []
    for iteration in range(2):
        block_full = lax.all_gather(current, "row", axis=1, tiled=True)
        projected = residue(lax.psum(forward_partial(block_full, tile_values, tile_cols), "col"))
        partial_term = backward_partial(projected, tile_values, onehot)
        applied = residue(lax.psum_scatter(partial_term, "row", scatter_dimension=1, tiled=True))
        current_own = current
        both_sums = lax.psum(
            jnp.stack(
                [
                    digit_pair(gram_local(current_own, applied)),
                    digit_pair(gram_local(applied, applied)),
                ]
            ),
            ("row", "col"),
        )
        gram_now = fold_digits(both_sums[0, 0], both_sums[0, 1])
        square_now = fold_digits(both_sums[1, 0], both_sums[1, 1])
        inverse_now = inverse_matrix(gram_now)
        coeffs = coefficients(
            gram_now, square_now, inverse_now, inverse_old, inverse_older, gram_old, square_old
        )
        stacked = jnp.concatenate([current, earlier, earliest], axis=0)
        following = residue(applied + combine_blocks(coeffs, stacked))
        results.append(following / modulus)
        earliest, earlier, current = (earlier, current, following)
        inverse_older, inverse_old = (inverse_old, inverse_now)
        gram_old, square_old = (gram_now, square_now)
    return (results[0], results[1])


def solution(mesh):
    placed = (
        P("row", "col", None, None),
        P("row", "col"),
        P(None, ("col", "row")),
        P(None, ("col", "row")),
        P(None, ("col", "row")),
        P(),
        P(),
        P(),
        P(),
    )
    return jax.shard_map(
        body,
        mesh=mesh,
        in_specs=placed,
        out_specs=(P(None, ("col", "row")), P(None, ("col", "row"))),
        check_vma=False,
    )
```

profile of v0, /device:TPU:1, one launch (start us, length us, event | category | flops | bytes accessed | tf_op | source)
XLA Modules:
  0.0 2244.6 jit_solution(948067549384732013)
XLA Ops:
  7.2 0.8 reshape.1652
  8.8 114.7 %all_gather.6 = f32[32,4096]{1,0:T(8,128)S(1)} all-gather(f32[32,128]{1,0:T(8,128)S(1)} %get-tuple-element.319), channel_id=1, replica_groups=mesh['row'=32,'col'=16] {'row'}, dimensions={1}, use_global_device_ids=true | all-gather | bytes 540672 | tf_op jit(solution)/shard_map/all_gather | solution.py:201
  124.9 0.8 copy_bitcast_fusion.7
  129.3 247.2 %all-reduce.3.cloned.1.call-done = f32[32,512]{1,0:T(8,128)} async-done(((f32[32,512]{1,0:T(8,128)}), f32[32,512]{1,0:T(8,128)}) %all-reduce.3.cloned.1.call-update) | async-done | bytes 65552 | tf_op jit(solution)/shard_map/psum | solution.py:202
  376.5 0.9 fusion.102
  378.1 1.1 convolution_bitcast_fusion.1
  379.2 1.1 add_select_fusion.22
  380.3 1.1 copy.355
  383.5 212.7 %reduce-scatter.3.cloned.1.call-done = f32[32,128]{1,0:T(8,128)} async-done(((f32[32,4096]{1,0:T(8,128)}), f32[32,128]{1,0:T(8,128)}) %reduce-scatter.3.cloned.1.call-update) | async-done | bytes 16400 | tf_op jit(solution)/shard_map/reduce_scatter | solution.py:204
  596.2 0.7 fusion.339
  597.5 125.4 %psum.29 = f32[2,2,32,32]{2,3,1,0:T(8,128)S(1)} all-reduce(f32[2,2,32,32]{2,3,1,0:T(8,128)S(1)} %pad_maximum_fusion.2), channel_id=1, replica_groups=mesh['row'=32,'col'=16] {'row','col'}, use_global_device_ids=true, to_apply=%region_2.4 | all-reduce | flops 4096 | bytes 32768 | tf_op jit(solution)/shard_map/psum | solution.py:206
  722.9 403.5 %while.36 = (s32[]{:T(128)}, f32[32,64]{0,1:T(8,128)S(1)}, s32[]{:T(128)}, s32[]{:T(128)}, s32[]{:T(128)}, /*index=5*/s32[]{:T(128)}, s32[]{:T(128)}, f32[]{:T(128)}, f32[]{:T(128)}, f32[]{:T(128)}, /*index=10*/f32[]{:T(128)}) while((s32[]{:T(128)}, f32[32,64]{0,1:T(8,128)S(1)}, s32[]{:T(128)}, s32[]{:T(128)}, ...), condition=%wide.region_6.8_spmd.clone.clone, body=%wide.region_3.7_spmd.clone.clone.sunk | while | flops 87498 | bytes 50118 | solution.py:82
  723.6 0.7 iota_reduce_fusion.4
  1129.8 103.1 %all_gather.7 = f32[32,4096]{1,0:T(8,128)S(1)} all-gather(f32[32,128]{1,0:T(8,128)S(1)} %get-tuple-element.280), channel_id=1, replica_groups=mesh['row'=32,'col'=16] {'row'}, dimensions={1}, use_global_device_ids=true | all-gather | bytes 540672 | tf_op jit(solution)/shard_map/all_gather | solution.py:201
  1234.2 0.8 copy_bitcast_fusion.6
  1235.6 249.9 %all-reduce.5.cloned.1.call-done = f32[32,512]{1,0:T(8,128)} async-done(((f32[32,512]{1,0:T(8,128)}), f32[32,512]{1,0:T(8,128)}) %all-reduce.5.cloned.1.call-update) | async-done | bytes 65552 | tf_op jit(solution)/shard_map/psum | solution.py:202
  1485.5 0.9 fusion.103
  1486.7 1.1 convolution_bitcast_fusion
  1487.7 1.1 add_select_fusion.18
  1488.9 1.1 copy.354
  1491.4 213.1 %reduce-scatter.5.cloned.1.call-done = f32[32,128]{1,0:T(8,128)} async-done(((f32[32,4096]{1,0:T(8,128)}), f32[32,128]{1,0:T(8,128)}) %reduce-scatter.5.cloned.1.call-update) | async-done | bytes 16400 | tf_op jit(solution)/shard_map/reduce_scatter | solution.py:204
  1704.5 0.7 fusion.343
  1705.8 125.7 %psum.31 = f32[2,2,32,32]{2,3,1,0:T(8,128)S(1)} all-reduce(f32[2,2,32,32]{2,3,1,0:T(8,128)S(1)} %pad_maximum_fusion.3), channel_id=1, replica_groups=mesh['row'=32,'col'=16] {'row','col'}, use_global_device_ids=true, to_apply=%region_9.11 | all-reduce | flops 4096 | bytes 32768 | tf_op jit(solution)/shard_map/psum | solution.py:206
  1831.6 403.5 %while.37 = (s32[]{:T(128)}, f32[32,64]{0,1:T(8,128)S(1)}, s32[]{:T(128)}, s32[]{:T(128)}, s32[]{:T(128)}, /*index=5*/s32[]{:T(128)}, s32[]{:T(128)}, f32[]{:T(128)}, f32[]{:T(128)}, f32[]{:T(128)}, /*index=10*/f32[]{:T(128)}) while((s32[]{:T(128)}, f32[32,64]{0,1:T(8,128)S(1)}, s32[]{:T(128)}, s32[]{:T(128)}, ...), condition=%wide.region_13.15_spmd.clone.clone, body=%wide.region_10.14_spmd.clone.clone.sunk | while | flops 87498 | bytes 50118 | solution.py:82
  (714 shorter events, 184.7 us)
Async XLA Ops:
  7.2 116.5 %copy-start = (s32[4,4,128,128]{3,2,1,0:T(8,128)S(1)}, s32[4,4,128,128]{3,2,1,0:T(8,128)}, u32[]{:S(2)}) copy-start(s32[4,4,128,128]{3,2,1,0:T(8,128)} %param.15) | copy-start | bytes 3145732
  7.2 369.3 %all-reduce.3.cloned.1.call-start = ((), (), s32[]{:S(2)}) async-start(), calls=%async_computation.2 | async-start | bytes 131072 | tf_op jit(solution)/shard_map/psum | solution.py:202
  125.7 0.7 copy-start.5
  125.7 0.8 copy-start.6
  125.7 470.4 %reduce-scatter.3.cloned.1.call-start = ((), (), s32[]{:S(2)}) async-start(), calls=%async_computation.3 | async-start | bytes 540672 | tf_op jit(solution)/shard_map/reduce_scatter | solution.py:204
  126.9 0.7 copy-start.7
  128.2 0.7 copy-start.8
  377.4 0.7 copy-start.4
  381.5 1104.0 %all-reduce.5.cloned.1.call-start = ((), (), s32[]{:S(2)}) async-start(), calls=%async_computation.4 | async-start | bytes 131072 | tf_op jit(solution)/shard_map/psum | solution.py:202
  382.0 0.7 copy-start.9
  382.0 0.7 copy-start.10
  382.8 0.7 copy-start.1
  1129.0 0.7 copy-start.2
  1235.0 469.5 %reduce-scatter.5.cloned.1.call-start = ((), (), s32[]{:S(2)}) async-start(), calls=%async_computation.5 | async-start | bytes 540672 | tf_op jit(solution)/shard_map/reduce_scatter | solution.py:204
  2236.6 0.7 copy-start.3
Sparse Core Ops, SparseCore 0:
  125.8 250.6 all-reduce.2
  381.6 214.5 reduce-scatter.2
  1235.1 250.3 all-reduce.4
  1490.1 214.3 reduce-scatter.4
where the time goes:
time: 2250 us; the launch traced here: 2240 us
  waiting for transfers between devices  923 us (41%)
  loops' own time  641 us (28%)
  blocking collectives  469 us (21%)
  other arithmetic  139 us (6%)
  local copies, waits for them, and re-layouts  47.5 us (2%)
    another operation x2, loops' own time, inverse_matrix(): augmented = lax.fori_loop(0, matrix_order, eliminate, augmented)  641 us
    psum x2, waiting for transfers between devices, body(): lax.psum(forward_partial(block_full, tile_values, tile_cols), 'col')  497 us
    reduce_scatter x2, waiting for transfers between devices, body(): lax.psum_scatter(partial_term, 'row', scatter_dimension=1, tiled=True)  426 us
    psum x2, blocking collectives, body(): lax.psum(jnp.stack([digit_pair(gram_local(current_own, applied)), digit_p...  251 us
    all_gather x2, blocking collectives, body(): block_full = lax.all_gather(current, 'row', axis=1, tiled=True)  218 us
    another operation x64, other arithmetic, eliminate(): pivot_row_id = jnp.where(jnp.any(usable), jnp.argmax(usable), column)  46.5 us
  transfers between devices with their start and end apart: 4, of which 4 were waited for; matrix products, arithmetic and copies ran while one was open for 0% of the time, Pallas kernels for 0%

commit v1 on v0

--- a/solution.py
+++ b/solution.py
@@ -199,7 +199,11 @@
     results = []
     for iteration in range(2):
         block_full = lax.all_gather(current, "row", axis=1, tiled=True)
-        projected = residue(lax.psum(forward_partial(block_full, tile_values, tile_cols), "col"))
+        projected = residue(
+            jnp.sum(
+                lax.all_gather(forward_partial(block_full, tile_values, tile_cols), "col"), axis=0
+            )
+        )
         partial_term = backward_partial(projected, tile_values, onehot)
         applied = residue(lax.psum_scatter(partial_term, "row", scatter_dimension=1, tiled=True))
         current_own = current

time: 2250 us -> 1910 us (0.85)
  waiting for transfers between devices: 923 us -> 575 us
    psum x2 -> x0, waiting for transfers between devices: 497 us -> none  [body(): lax.psum(forward_partial(block_full, tile_values, tile_cols), 'col')]
    all_gather x0 -> x2, waiting for transfers between devices: none -> 168 us  [body(): lax.all_gather(forward_partial(block_full, tile_values, tile_cols), 'col')]
where the time goes in v1:
time: 1910 us
  loops' own time  648 us (34%)
  waiting for transfers between devices  575 us (30%)
  blocking collectives  469 us (25%)
  other arithmetic  140 us (7%)
  local copies, waits for them, and re-layouts  51.6 us (3%)
    another operation x2, loops' own time, inverse_matrix(): augmented = lax.fori_loop(0, matrix_order, eliminate, augmented)  648 us
    reduce_scatter x2, waiting for transfers between devices, body(): lax.psum_scatter(partial_term, 'row', scatter_dimension=1, tiled=True)  407 us
    psum x2, blocking collectives, body(): lax.psum(jnp.stack([digit_pair(gram_local(current_own, applied)), digit_p...  251 us
    all_gather x2, blocking collectives, body(): block_full = lax.all_gather(current, 'row', axis=1, tiled=True)  217 us
    all_gather x2, waiting for transfers between devices, body(): lax.all_gather(forward_partial(block_full, tile_values, tile_cols), 'col')  168 us
    another operation x64, other arithmetic, eliminate(): pivot_row_id = jnp.where(jnp.any(usable), jnp.argmax(usable), column)  44.7 us
    eq x64, other arithmetic, eliminate(): return jnp.where((row_numbers == column)[:, None], scaled[None, :], reduced)  43.8 us
    dynamic_slice x64, local copies, waits for them, and re-layouts, eliminate(): scaled = mulmod(pivot_row, inverse_scalar(pivot_row[column]))  40.2 us
  transfers between devices with their start and end apart: 4, of which 4 were waited for; matrix products, arithmetic and copies ran while one was open for 0% of the time, Pallas kernels for 0%

profile of v1, /device:TPU:1, one launch (start us, length us, event | category | flops | bytes accessed | tf_op | source)
XLA Modules:
  0.0 1908.0 jit_solution(9665272047162300574)
XLA Ops:
  7.2 0.8 reshape.1650
  8.8 114.7 %all_gather.12 = f32[32,4096]{1,0:T(8,128)S(1)} all-gather(f32[32,128]{1,0:T(8,128)S(1)} %get-tuple-element.319), channel_id=1, replica_groups=mesh['row'=32,'col'=16] {'row'}, dimensions={1}, use_global_device_ids=true | all-gather | bytes 540672 | tf_op jit(solution)/shard_map/all_gather | solution.py:201
  129.6 82.9 %all-gather.3.cloned.1.call-done = f32[16,32,512]{2,1,0:T(8,128)} async-done(((f32[1,32,512]{2,1,0:T(8,128)}), f32[16,32,512]{2,1,0:T(8,128)}) %all-gather.3.cloned.1.call-update) | async-done | bytes 1048592 | tf_op jit(solution)/shard_map/all_gather | solution.py:204
  212.4 1.3 reduce_sum.16
  214.5 1.1 convolution_bitcast_fusion.1
  215.5 1.1 add_select_fusion.22
  216.7 1.1 copy.300
  219.8 203.0 %reduce-scatter.3.cloned.1.call-done = f32[32,128]{1,0:T(8,128)} async-done(((f32[32,4096]{1,0:T(8,128)}), f32[32,128]{1,0:T(8,128)}) %reduce-scatter.3.cloned.1.call-update) | async-done | bytes 16400 | tf_op jit(solution)/shard_map/reduce_scatter | solution.py:208
  422.8 0.7 fusion.335
  424.1 125.7 %psum.14 = f32[2,2,32,32]{2,3,1,0:T(8,128)S(1)} all-reduce(f32[2,2,32,32]{2,3,1,0:T(8,128)S(1)} %pad_maximum_fusion.2), channel_id=1, replica_groups=mesh['row'=32,'col'=16] {'row','col'}, use_global_device_ids=true, to_apply=%region_2.4 | all-reduce | flops 4096 | bytes 32768 | tf_op jit(solution)/shard_map/psum | solution.py:210
  550.0 403.5 %while.36 = (s32[]{:T(128)}, f32[32,64]{0,1:T(8,128)S(1)}, s32[]{:T(128)}, s32[]{:T(128)}, s32[]{:T(128)}, /*index=5*/s32[]{:T(128)}, s32[]{:T(128)}, f32[]{:T(128)}, f32[]{:T(128)}, f32[]{:T(128)}, /*index=10*/f32[]{:T(128)}) while((s32[]{:T(128)}, f32[32,64]{0,1:T(8,128)S(1)}, s32[]{:T(128)}, s32[]{:T(128)}, ...), condition=%wide.region_6.8_spmd.clone.clone, body=%wide.region_3.7_spmd.clone.clone.sunk | while | flops 87498 | bytes 50118 | solution.py:82
  550.7 0.7 iota_reduce_fusion.4
  563.3 0.7 iota_reduce_fusion.4
  575.9 0.7 iota_reduce_fusion.4
  955.9 102.5 %all_gather.14 = f32[32,4096]{1,0:T(8,128)S(1)} all-gather(f32[32,128]{1,0:T(8,128)S(1)} %get-tuple-element.280), channel_id=1, replica_groups=mesh['row'=32,'col'=16] {'row'}, dimensions={1}, use_global_device_ids=true | all-gather | bytes 540672 | tf_op jit(solution)/shard_map/all_gather | solution.py:201
  1062.1 85.4 %all-gather.5.cloned.1.call-done = f32[16,32,512]{2,1,0:T(8,128)} async-done(((f32[1,32,512]{2,1,0:T(8,128)}), f32[16,32,512]{2,1,0:T(8,128)}) %all-gather.5.cloned.1.call-update) | async-done | bytes 1048592 | tf_op jit(solution)/shard_map/all_gather | solution.py:204
  1147.5 1.3 reduce_sum.20
  1149.0 1.1 convolution_bitcast_fusion
  1150.1 1.1 add_select_fusion.18
  1151.3 1.1 copy.299
  1153.7 203.7 %reduce-scatter.5.cloned.1.call-done = f32[32,128]{1,0:T(8,128)} async-done(((f32[32,4096]{1,0:T(8,128)}), f32[32,128]{1,0:T(8,128)}) %reduce-scatter.5.cloned.1.call-update) | async-done | bytes 16400 | tf_op jit(solution)/shard_map/reduce_scatter | solution.py:208
  1357.4 0.7 fusion.339
  1358.7 125.7 %psum.15 = f32[2,2,32,32]{2,3,1,0:T(8,128)S(1)} all-reduce(f32[2,2,32,32]{2,3,1,0:T(8,128)S(1)} %pad_maximum_fusion.3), channel_id=1, replica_groups=mesh['row'=32,'col'=16] {'row','col'}, use_global_device_ids=true, to_apply=%region_9.11 | all-reduce | flops 4096 | bytes 32768 | tf_op jit(solution)/shard_map/psum | solution.py:210
  1484.6 413.9 %while.37 = (s32[]{:T(128)}, f32[32,64]{0,1:T(8,128)S(1)}, s32[]{:T(128)}, s32[]{:T(128)}, s32[]{:T(128)}, /*index=5*/s32[]{:T(128)}, s32[]{:T(128)}, f32[]{:T(128)}, f32[]{:T(128)}, f32[]{:T(128)}, /*index=10*/f32[]{:T(128)}) while((s32[]{:T(128)}, f32[32,64]{0,1:T(8,128)S(1)}, s32[]{:T(128)}, s32[]{:T(128)}, ...), condition=%wide.region_13.15_spmd.clone.clone, body=%wide.region_10.14_spmd.clone.clone.sunk | while | flops 87498 | bytes 50118 | solution.py:82
  (716 shorter events, 188.6 us)
Async XLA Ops:
  7.2 116.5 %copy-start = (s32[4,4,128,128]{3,2,1,0:T(8,128)S(1)}, s32[4,4,128,128]{3,2,1,0:T(8,128)}, u32[]{:S(2)}) copy-start(s32[4,4,128,128]{3,2,1,0:T(8,128)} %param.15) | copy-start | bytes 3145732
  7.2 205.2 %all-gather.3.cloned.1.call-start = ((), (), s32[]{:S(2)}) async-start(), calls=%async_computation.2 | async-start | bytes 1114112 | tf_op jit(solution)/shard_map/all_gather | solution.py:204
  125.8 0.7 copy-start.5
  125.8 0.8 copy-start.6
  125.8 297.0 %reduce-scatter.3.cloned.1.call-start = ((), (), s32[]{:S(2)}) async-start(), calls=%async_computation.3 | async-start | bytes 540672 | tf_op jit(solution)/shard_map/reduce_scatter | solution.py:208
  126.6 0.7 copy-start.7
  127.3 0.7 copy-start.8
  213.8 0.7 copy-start.4
  217.8 929.7 %all-gather.5.cloned.1.call-start = ((), (), s32[]{:S(2)}) async-start(), calls=%async_computation.4 | async-start | bytes 1114112 | tf_op jit(solution)/shard_map/all_gather | solution.py:204
  218.4 0.7 copy-start.9
  218.4 0.7 copy-start.10
  219.1 0.7 copy-start.1
  955.1 0.7 copy-start.3
  1060.6 296.9 %reduce-scatter.5.cloned.1.call-start = ((), (), s32[]{:S(2)}) async-start(), calls=%async_computation.5 | async-start | bytes 540672 | tf_op jit(solution)/shard_map/reduce_scatter | solution.py:208
  1900.0 0.7 copy-start.2
Sparse Core Ops, SparseCore 0:
  125.9 86.4 all-gather.2
  217.9 204.8 reduce-scatter.2
  1060.7 86.7 all-gather.4
  1152.5 204.8 reduce-scatter.4
